TPU v7x, 256 devices: a whole 4x4x8 slice. The times are simulated.
256 devices in a mesh: seq: 64 (over y_lo, x, z), dp: 4 (over y_hi, core).
Axes of the slice: x: 4, y: 4 (y_hi: 2, y_lo: 2; y = y_hi * 2 + y_lo), z: 8, core: 2. Of those that a mesh axis runs over, the one named last changes fastest.
Arguments:
- signal: float32 [4, 65536, 384], P('dp', 'seq'), may hold values from -6 to 6
- gate_values: float32 [4, 65536, 384], P('dp', 'seq'), may hold values from -6 to 6
- cotangent: float32 [4, 65536, 384], P('dp', 'seq'), may hold values from -6 to 6
- kernel: float32 [128, 512, 384], P(None, 'seq'), may hold values from -6 to 6
- first_factor: float32 [128, 128], replicated, may hold values from -0.5 to 0.5
- second_factor: float32 [512, 512], replicated, may hold values from -0.25 to 0.25
Outputs:
- grad_signal: float32 [4, 65536, 384], P('dp', 'seq')
- grad_gates: float32 [4, 65536, 384], P('dp', 'seq')
- grad_kernel: float32 [128, 512, 384], P('dp', 'seq')
- grad_first: float32 [128, 128], replicated
- grad_second: float32 [512, 512], replicated
All inputs are finite; a program needn't handle non-finite values.
Results may differ from a plain program's by a relative error of at most 0.000071.
Values sent between devices are 32-bit elements; how exact they have to be, the bound alone decides.
No kernel may reach another device: no remote copies, remote signals or barrier semaphores. Data moves between devices by JAX's collectives and lax.ppermute only.
A program may use at most 128 MiB of HBM per device.

v0:
```python
import math
import jax
import jax.numpy as jnp
from jax import lax
from jax.sharding import PartitionSpec as P


def along_second(data, factor):
    return jnp.einsum("bijc,kj->bikc", data, factor, precision=lax.Precision.HIGHEST)


def along_second_t(data, factor):
    return jnp.einsum("bikc,kj->bijc", data, factor, precision=lax.Precision.HIGHEST)


def along_first(factor, data):
    return jnp.einsum("mi,bikc->bmkc", factor, data, precision=lax.Precision.HIGHEST)


def along_first_t(factor, data):
    return jnp.einsum("mi,bmkc->bikc", factor, data, precision=lax.Precision.HIGHEST)


def outer_first(left, right):
    return jnp.einsum("bmkc,bikc->mi", left, right, precision=lax.Precision.HIGHEST)


def outer_second(left, right):
    return jnp.einsum("bikc,bijc->kj", left, right, precision=lax.Precision.HIGHEST)


def body(signal, gate_values, cotangent, kernel, first_factor, second_factor):
    batch = signal.shape[0]
    blocks = first_factor.shape[0]
    block = second_factor.shape[0]
    channels = signal.shape[2]
    local_rows = signal.shape[1] // block
    shape_rows = (batch, local_rows, block, channels)
    source = signal.reshape(shape_rows)
    gating = gate_values.reshape(shape_rows)
    upstream = cotangent.reshape(shape_rows)
    whole = lax.all_to_all(source, "seq", split_axis=3, concat_axis=1, tiled=True)
    kernel_cols = lax.all_to_all(kernel, "seq", split_axis=2, concat_axis=1, tiled=True)
    section_one = along_second(whole, second_factor)
    spectrum = along_first(first_factor, section_one)
    weighted = kernel_cols[None] * spectrum
    back_one = along_first_t(first_factor, weighted)
    full_mixed = along_second_t(back_one, second_factor)
    mixed = lax.all_to_all(full_mixed, "seq", split_axis=1, concat_axis=3, tiled=True)
    grad_mixed = upstream * gating
    grad_gate = upstream * mixed
    grad_whole = lax.all_to_all(grad_mixed, "seq", split_axis=3, concat_axis=1, tiled=True)
    grad_back = along_second(grad_whole, second_factor)
    second_grad = outer_second(back_one, grad_whole)
    grad_weighted = along_first(first_factor, grad_back)
    first_grad = outer_first(weighted, grad_back)
    kernel_cols_grad = jnp.sum(grad_weighted * spectrum, axis=0)
    grad_spectrum = grad_weighted * kernel_cols[None]
    grad_section = along_first_t(first_factor, grad_spectrum)
    first_grad = first_grad + outer_first(grad_spectrum, section_one)
    grad_full = along_second_t(grad_section, second_factor)
    second_grad = second_grad + outer_second(grad_section, whole)
    grad_source = lax.all_to_all(grad_full, "seq", split_axis=1, concat_axis=3, tiled=True)
    kernel_term = lax.all_to_all(kernel_cols_grad, "seq", split_axis=1, concat_axis=2, tiled=True)
    grad_kernel = lax.psum_scatter(kernel_term, "dp", scatter_dimension=0, tiled=True)
    first_total, second_total = lax.psum((first_grad, second_grad), ("seq", "dp"))
    sequences = batch * lax.axis_size("dp")
    first_scale = 1.0 / math.sqrt(sequences * block * channels)
    second_scale = 1.0 / math.sqrt(sequences * blocks * channels)
    return (
        grad_source.reshape(signal.shape),
        grad_gate.reshape(signal.shape),
        grad_kernel,
        first_total * first_scale,
        second_total * second_scale,
    )


def solution(mesh):
    in_specs = (
        P("dp", "seq", None),
        P("dp", "seq", None),
        P("dp", "seq", None),
        P(None, "seq", None),
        P(),
        P(),
    )
    out_specs = (P("dp", "seq", None), P("dp", "seq", None), P("dp", "seq", None), P(), P())
    return jax.shard_map(body, mesh=mesh, in_specs=in_specs, out_specs=out_specs, check_vma=False)
```

profile of v0, /device:TPU:6, one launch (start us, length us, event | category | flops | bytes accessed | tf_op | source)
XLA Modules:
  0.0 535.5 jit_solution(2666855981043520354)
XLA Ops:
  8.0 0.0 copy-start
  8.0 3.8 copy.114
  11.8 13.0 %all-to-all-start.3 = ((f32[1,2,512,384]{2,1,0,3:T(2,128)}), f32[1,2,512,384]{2,1,0,3:T(2,128)S(1)}, u32[]{:S(2)}, u32[]{:S(2)}) async-start(f32[1,2,512,384]{2,1,0,3:T(2,128)} %copy.114), calls=%async_computation.3 | async-start | bytes 3145728 | tf_op jit(solution)/shard_map/all_to_all | solution.py:42
  24.8 3.2 mul.41
  28.0 3.7 copy.113
  31.7 32.9 %all-to-all-done.3 = f32[1,2,512,384]{2,1,0,3:T(2,128)S(1)} async-done(((f32[1,2,512,384]{2,1,0,3:T(2,128)}), f32[1,2,512,384]{2,1,0,3:T(2,128)S(1)}, u32[]{:S(2)}, u32[]{:S(2)}) %all-to-all-start.3) | async-done | bytes 1572896 | tf_op jit(solution)/shard_map/all_to_all | solution.py:42
  64.6 6.6 %all-to-all-start = ((f32[1,2,512,384]{2,1,0,3:T(2,128)}), f32[1,2,512,384]{2,1,0,3:T(2,128)}, u32[]{:S(2)}, u32[]{:S(2)}) async-start(f32[1,2,512,384]{2,1,0,3:T(2,128)} %copy.113), calls=%async_computation | async-start | bytes 3145728 | tf_op jit(solution)/shard_map/all_to_all | solution.py:52
  71.2 3.1 copy.87
  74.3 35.7 %all-to-all-done = f32[1,2,512,384]{2,1,0,3:T(2,128)} async-done(((f32[1,2,512,384]{2,1,0,3:T(2,128)}), f32[1,2,512,384]{2,1,0,3:T(2,128)}, u32[]{:S(2)}, u32[]{:S(2)}) %all-to-all-start) | async-done | bytes 1572896 | tf_op jit(solution)/shard_map/all_to_all | solution.py:52
  110.0 6.3 %all-to-all-start.1 = ((f32[128,8,384]{0,1,2:T(8,128)}), f32[128,8,384]{0,1,2:T(8,128)S(1)}, u32[]{:S(2)}, u32[]{:S(2)}) async-start(f32[128,8,384]{0,1,2:T(8,128)} %copy.87), calls=%async_computation.1 | async-start | bytes 3145728 | tf_op jit(solution)/shard_map/all_to_all | solution.py:43
  116.3 3.1 copy.93
  119.4 3.1 reshape.99
  122.5 3.1 copy.85
  125.6 3.3 reshape.93
  128.9 0.0 copy-start.15
  129.0 4.2 fusion.44
  133.2 0.0 copy-done.15
  133.2 0.0 copy-start.8
  133.2 1.5 fusion.10
  134.7 0.5 copy-done.8
  135.2 2.7 fusion.47
  137.9 2.6 fusion.14
  140.5 0.0 copy-start.1
  140.5 0.2 fusion.17
  140.7 1.0 copy-done.1
  141.6 2.2 copy.98
  143.9 10.8 %all-to-all-done.1 = f32[128,8,384]{0,1,2:T(8,128)S(1)} async-done(((f32[128,8,384]{0,1,2:T(8,128)}), f32[128,8,384]{0,1,2:T(8,128)S(1)}, u32[]{:S(2)}, u32[]{:S(2)}) %all-to-all-start.1) | async-done | bytes 1572896 | tf_op jit(solution)/shard_map/all_to_all | solution.py:43
  154.6 6.9 %all-to-all-start.5 = ((f32[128,512,6]{0,2,1:T(8,128)}), f32[128,512,6]{0,2,1:T(8,128)}, u32[]{:S(2)}, u32[]{:S(2)}) async-start(f32[128,512,6]{0,2,1:T(8,128)} %copy.98), calls=%async_computation.5 | async-start | bytes 4194304 | tf_op jit(solution)/shard_map/all_to_all | solution.py:64
  161.5 2.8 fusion.53
  164.3 1.2 copy-done.13
  165.5 2.7 fusion.19
  168.2 2.9 copy.95
  171.1 38.3 %all-to-all-done.5 = f32[128,512,6]{0,2,1:T(8,128)} async-done(((f32[128,512,6]{0,2,1:T(8,128)}), f32[128,512,6]{0,2,1:T(8,128)}, u32[]{:S(2)}, u32[]{:S(2)}) %all-to-all-start.5) | async-done | bytes 1572896 | tf_op jit(solution)/shard_map/all_to_all | solution.py:64
  209.4 6.8 %all-to-all-start.4 = ((f32[1,128,512,6]{2,0,3,1:T(1,128)}), f32[1,128,512,6]{2,0,3,1:T(1,128)}, u32[]{:S(2)}, u32[]{:S(2)}) async-start(f32[1,128,512,6]{2,0,3,1:T(1,128)} %copy.95), calls=%async_computation.4 | async-start | bytes 3145728 | tf_op jit(solution)/shard_map/all_to_all | solution.py:49
  216.2 0.4 all-reduce.3.cloned.1.call-start
  216.6 4.7 fusion.25
  221.4 0.0 copy-start.2
  221.4 2.7 fusion.34
  224.1 1.4 fusion.50
  225.6 0.0 copy-start.11
  225.6 3.4 fusion.40
  229.0 3.7 fusion.31
  232.7 0.0 all-reduce.3.cloned.1.call-update
  232.7 0.2 reduce-scatter.2.cloned.1.call-start
  232.9 1.9 copy.100
  234.9 1.8 copy.101
  236.7 0.0 reduce-scatter.2.cloned.1.call-update
  236.7 1.4 copy-done.12
  238.1 2.7 fusion.22
  240.7 2.8 copy.90
  243.5 9.3 %all-to-all-done.4 = f32[1,128,512,6]{2,0,3,1:T(1,128)} async-done(((f32[1,128,512,6]{2,0,3,1:T(1,128)}), f32[1,128,512,6]{2,0,3,1:T(1,128)}, u32[]{:S(2)}, u32[]{:S(2)}) %all-to-all-start.4) | async-done | bytes 1572896 | tf_op jit(solution)/shard_map/all_to_all | solution.py:49
  252.7 6.8 %all-to-all-start.2 = ((f32[1,128,512,6]{2,0,3,1:T(1,128)}), f32[1,128,512,6]{2,0,3,1:T(1,128)S(1)}, u32[]{:S(2)}, u32[]{:S(2)}) async-start(f32[1,128,512,6]{2,0,3,1:T(1,128)} %copy.90), calls=%async_computation.2 | async-start | bytes 3145728 | tf_op jit(solution)/shard_map/all_to_all | solution.py:63
  259.6 3.0 copy.97
  262.6 242.0 %all-reduce.3.cloned.1.call-done = (f32[128,128]{1,0:T(8,128)}, f32[512,512]{1,0:T(8,128)}) async-done(((f32[128,128]{1,0:T(8,128)}, f32[512,512]{1,0:T(8,128)}), (f32[128,128]{1,0:T(8,128)}, f32[512,512]{1,0:T(8,128)})) %all-reduce.3.cloned.1.call-update) | async-done | bytes 1114128 | tf_op jit(solution)/shard_map/psum | solution.py:66
  504.6 1.5 broadcast_multiply_fusion.1
  506.1 2.3 broadcast_multiply_fusion
  508.4 3.4 copy.124
  511.8 3.4 all_to_all.85
  515.2 3.4 mul.45
  518.6 3.0 copy.106
  521.6 0.0 all-to-all-done.2
  521.6 2.0 copy.125
  523.5 2.6 reshape.97
  526.2 1.6 copy.105
  (22 shorter events, 0.0 us)
Async XLA Ops:
  8.0 120.9 %copy-start = (f32[512,512]{1,0:T(8,128)S(1)}, f32[512,512]{1,0:T(8,128)}, u32[]{:S(2)}) copy-start(f32[512,512]{1,0:T(8,128)} %param.11) | copy-start | bytes 3145732
  11.8 52.8 %all-to-all-start.3 = ((f32[1,2,512,384]{2,1,0,3:T(2,128)}), f32[1,2,512,384]{2,1,0,3:T(2,128)S(1)}, u32[]{:S(2)}, u32[]{:S(2)}) async-start(f32[1,2,512,384]{2,1,0,3:T(2,128)} %copy.114), calls=%async_computation.3 | async-start | bytes 3145728 | tf_op jit(solution)/shard_map/all_to_all | solution.py:42
  64.6 9.7 %copy-start.14 = (f32[1,2,512,384]{2,1,0,3:T(2,128)}, f32[1,2,512,384]{2,1,0,3:T(2,128)S(1)}, u32[]{:S(2)}) copy-start(f32[1,2,512,384]{2,1,0,3:T(2,128)S(1)} %all-to-all-done.3) | copy-start | bytes 4718596
  64.6 45.4 %all-to-all-start = ((f32[1,2,512,384]{2,1,0,3:T(2,128)}), f32[1,2,512,384]{2,1,0,3:T(2,128)}, u32[]{:S(2)}, u32[]{:S(2)}) async-start(f32[1,2,512,384]{2,1,0,3:T(2,128)} %copy.113), calls=%async_computation | async-start | bytes 3145728 | tf_op jit(solution)/shard_map/all_to_all | solution.py:52
  110.0 44.6 %all-to-all-start.1 = ((f32[128,8,384]{0,1,2:T(8,128)}), f32[128,8,384]{0,1,2:T(8,128)S(1)}, u32[]{:S(2)}, u32[]{:S(2)}) async-start(f32[128,8,384]{0,1,2:T(8,128)} %copy.87), calls=%async_computation.1 | async-start | bytes 3145728 | tf_op jit(solution)/shard_map/all_to_all | solution.py:43
  128.9 4.2 copy-start.15
  133.2 1.5 copy-start.6
  133.2 2.0 copy-start.8
  135.2 5.3 copy-start.3
  137.8 2.6 copy-start.9
  140.5 1.1 copy-start.1
  154.6 54.7 %all-to-all-start.5 = ((f32[128,512,6]{0,2,1:T(8,128)}), f32[128,512,6]{0,2,1:T(8,128)}, u32[]{:S(2)}, u32[]{:S(2)}) async-start(f32[128,512,6]{0,2,1:T(8,128)} %copy.98), calls=%async_computation.5 | async-start | bytes 4194304 | tf_op jit(solution)/shard_map/all_to_all | solution.py:64
  164.3 1.2 copy-start.13
  209.4 43.4 %all-to-all-start.4 = ((f32[1,128,512,6]{2,0,3,1:T(1,128)}), f32[1,128,512,6]{2,0,3,1:T(1,128)}, u32[]{:S(2)}, u32[]{:S(2)}) async-start(f32[1,128,512,6]{2,0,3,1:T(1,128)} %copy.95), calls=%async_computation.4 | async-start | bytes 3145728 | tf_op jit(solution)/shard_map/all_to_all | solution.py:49
  216.2 288.4 %all-reduce.3.cloned.1.call-start = ((), (), s32[]{:S(2)}) async-start(), calls=%async_computation.8 | async-start | bytes 2228224 | tf_op jit(solution)/shard_map/psum | solution.py:66
  216.6 4.7 copy-start.4
  216.6 4.7 copy-start.10
  221.4 2.7 copy-start.2
  224.1 1.4 copy-start.7
  225.6 3.4 copy-start.11
  225.6 3.4 copy-start.5
  232.7 295.1 %reduce-scatter.2.cloned.1.call-start = ((), (), s32[]{:S(2)}) async-start(), calls=%async_computation.7 | async-start | bytes 1966080 | tf_op jit(solution)/shard_map/reduce_scatter | solution.py:65
  236.7 1.4 copy-start.12
  252.7 268.8 %all-to-all-start.2 = ((f32[1,128,512,6]{2,0,3,1:T(1,128)}), f32[1,128,512,6]{2,0,3,1:T(1,128)S(1)}, u32[]{:S(2)}, u32[]{:S(2)}) async-start(f32[1,128,512,6]{2,0,3,1:T(1,128)} %copy.90), calls=%async_computation.2 | async-start | bytes 3145728 | tf_op jit(solution)/shard_map/all_to_all | solution.py:63
Sparse Core Ops, SparseCore 0:
  232.8 271.7 all-reduce.2
Sparse Core Ops, SparseCore 1:
  236.8 48.6 reduce-scatter.1
where the time goes:
time: 543 us; the launch traced here: 535 us
  waiting for transfers between devices  369 us (68%)
  local copies, waits for them, and re-layouts  57.9 us (11%)
  starting transfers between devices  47 us (9%)
  matrix products  35 us (6%)
  between operations  16 us (3%)
  other arithmetic  10.5 us (2%)
    psum x1, waiting for transfers between devices, body(): lax.psum((first_grad, second_grad), ('seq', 'dp'))  242 us
    all_to_all x1, waiting for transfers between devices, body(): lax.all_to_all(kernel_cols_grad, 'seq', split_axis=1, concat_axis=2, tile...  38.3 us
    all_to_all x1, waiting for transfers between devices, body(): lax.all_to_all(grad_mixed, 'seq', split_axis=3, concat_axis=1, tiled=True)  35.7 us
    all_to_all x1, waiting for transfers between devices, body(): lax.all_to_all(source, 'seq', split_axis=3, concat_axis=1, tiled=True)  32.9 us
    unnamed x36, local copies, waits for them, and re-layouts  14.9 us
    all_to_all x1, starting transfers between devices, body(): lax.all_to_all(source, 'seq', split_axis=3, concat_axis=1, tiled=True)  13 us
  transfers between devices with their start and end apart: 8, of which 6 were waited for; matrix products, arithmetic and copies ran while one was open for 17% of the time, Pallas kernels for 0%

commit v1 on v0

--- a/solution.py
+++ b/solution.py
@@ -1,8 +1,16 @@
+import functools
 import math
 import jax
 import jax.numpy as jnp
 from jax import lax
 from jax.sharding import PartitionSpec as P
+
+
+def copies_trace(obj, net_axis, ax_name):
+    return lax.psum(lax.psum(obj, net_axis), ax_name)
+
+
+set_spans = functools.partial(copies_trace, net_axis="seq", ax_name="dp")
 
 
 def along_second(data, factor):
@@ -63,7 +71,7 @@
     grad_source = lax.all_to_all(grad_full, "seq", split_axis=1, concat_axis=3, tiled=True)
     kernel_term = lax.all_to_all(kernel_cols_grad, "seq", split_axis=1, concat_axis=2, tiled=True)
     grad_kernel = lax.psum_scatter(kernel_term, "dp", scatter_dimension=0, tiled=True)
-    first_total, second_total = lax.psum((first_grad, second_grad), ("seq", "dp"))
+    first_total, second_total = set_spans((first_grad, second_grad))
     sequences = batch * lax.axis_size("dp")
     first_scale = 1.0 / math.sqrt(sequences * block * channels)
     second_scale = 1.0 / math.sqrt(sequences * blocks * channels)

time: 543 us -> 922 us (1.70)
  waiting for transfers between devices: 369 us -> 740 us
  starting transfers between devices: 47 us -> 57.7 us
    psum x1 -> x2, waiting for transfers between devices: 242 us -> 607 us  [copies_trace(): return lax.psum(lax.psum(obj, net_axis), ax_name)]
    reduce_scatter x1, waiting for transfers between devices: 0.01 us -> 20.5 us  [body(): lax.psum_scatter(kernel_term, 'dp', scatter_dimension=0, tiled=True)]
    all_to_all x1, starting transfers between devices: 6.81 us -> 17.9 us  [body(): lax.all_to_all(grad_full, 'seq', split_axis=1, concat_axis=3, tiled=True)]
    all_to_all x1, waiting for transfers between devices: 9.26 us -> 0.01 us  [body(): lax.all_to_all(full_mixed, 'seq', split_axis=1, concat_axis=3, tiled=True)]
  transfers between devices with their start and end apart: 8 -> 9, of which waited for: 6 -> 7; matrix products, arithmetic and copies ran while one was open for 17% -> 10% of each run, Pallas kernels for 0% -> 0%
where the time goes in v1:
time: 922 us; the launch traced here: 914 us
  waiting for transfers between devices  740 us (80%)
  local copies, waits for them, and re-layouts  57.8 us (6%)
  starting transfers between devices  57.7 us (6%)
  matrix products  34.5 us (4%)
  between operations  14.3 us (2%)
  other arithmetic  10.5 us (1%)
    psum x2, waiting for transfers between devices, copies_trace(): return lax.psum(lax.psum(obj, net_axis), ax_name)  607 us
    all_to_all x1, waiting for transfers between devices, body(): lax.all_to_all(grad_mixed, 'seq', split_axis=3, concat_axis=1, tiled=True)  35.8 us
    all_to_all x1, waiting for transfers between devices, body(): lax.all_to_all(source, 'seq', split_axis=3, concat_axis=1, tiled=True)  32.9 us
    all_to_all x1, waiting for transfers between devices, body(): lax.all_to_all(kernel_cols_grad, 'seq', split_axis=1, concat_axis=2, tile...  32.3 us
    reduce_scatter x1, waiting for transfers between devices, body(): lax.psum_scatter(kernel_term, 'dp', scatter_dimension=0, tiled=True)  20.5 us
  transfers between devices with their start and end apart: 9, of which 7 were waited for; matrix products, arithmetic and copies ran while one was open for 10% of the time, Pallas kernels for 0%

profile of v1, /device:TPU:6, one launch (start us, length us, event | category | flops | bytes accessed | tf_op | source)
XLA Modules:
  0.0 914.4 jit_solution(13545571677379559737)
XLA Ops:
  7.2 0.0 copy-start
  7.2 3.8 copy.114
  10.9 13.0 %all-to-all-start.3 = ((f32[1,2,512,384]{2,1,0,3:T(2,128)}), f32[1,2,512,384]{2,1,0,3:T(2,128)S(1)}, u32[]{:S(2)}, u32[]{:S(2)}) async-start(f32[1,2,512,384]{2,1,0,3:T(2,128)} %copy.114), calls=%async_computation.3 | async-start | bytes 3145728 | tf_op jit(solution)/shard_map/all_to_all | solution.py:50
  24.0 3.2 mul.41
  27.1 3.7 copy.113
  30.8 32.9 %all-to-all-done.3 = f32[1,2,512,384]{2,1,0,3:T(2,128)S(1)} async-done(((f32[1,2,512,384]{2,1,0,3:T(2,128)}), f32[1,2,512,384]{2,1,0,3:T(2,128)S(1)}, u32[]{:S(2)}, u32[]{:S(2)}) %all-to-all-start.3) | async-done | bytes 1572896 | tf_op jit(solution)/shard_map/all_to_all | solution.py:50
  63.7 6.6 all-to-all-start
  70.3 3.0 copy.87
  73.4 35.8 %all-to-all-done = f32[1,2,512,384]{2,1,0,3:T(2,128)} async-done(((f32[1,2,512,384]{2,1,0,3:T(2,128)}), f32[1,2,512,384]{2,1,0,3:T(2,128)}, u32[]{:S(2)}, u32[]{:S(2)}) %all-to-all-start) | async-done | bytes 1572896 | tf_op jit(solution)/shard_map/all_to_all | solution.py:60
  109.2 6.3 all-to-all-start.1
  115.5 3.1 copy.93
  118.5 3.1 reshape.99
  121.7 3.1 copy.85
  124.8 3.3 reshape.93
  128.1 0.0 copy-start.17
  128.1 4.2 fusion.44
  132.3 0.0 copy-start.6
  132.3 1.5 fusion.10
  133.8 0.5 copy-done.6
  134.3 2.7 fusion.47
  137.0 2.6 fusion.14
  139.6 0.0 copy-start.1
  139.7 0.2 fusion.17
  139.8 1.0 copy-done.1
  140.8 2.3 copy.98
  143.1 10.7 %all-to-all-done.1 = f32[128,8,384]{0,1,2:T(8,128)S(1)} async-done(((f32[128,8,384]{0,1,2:T(8,128)}), f32[128,8,384]{0,1,2:T(8,128)S(1)}, u32[]{:S(2)}, u32[]{:S(2)}) %all-to-all-start.1) | async-done | bytes 1572896 | tf_op jit(solution)/shard_map/all_to_all | solution.py:51
  153.8 6.9 all-to-all-start.5
  160.7 2.8 fusion.53
  163.5 1.2 copy-done.14
  164.7 2.7 fusion.19
  167.4 2.8 copy.95
  170.2 2.6 fusion.34
  172.9 3.4 fusion.40
  176.2 32.3 %all-to-all-done.5 = f32[128,512,6]{0,2,1:T(8,128)} async-done(((f32[128,512,6]{0,2,1:T(8,128)}), f32[128,512,6]{0,2,1:T(8,128)}, u32[]{:S(2)}, u32[]{:S(2)}) %all-to-all-start.5) | async-done | bytes 1572896 | tf_op jit(solution)/shard_map/all_to_all | solution.py:72
  208.5 6.8 all-to-all-start.4
  215.3 0.0 all-reduce.5.cloned.1.call-start
  215.4 0.0 copy-start.7
  215.4 3.0 fusion.50
  218.4 2.7 fusion.25
  221.1 3.7 fusion.31
  224.8 0.0 all-reduce.5.cloned.1.call-update
  224.8 0.0 all-reduce.7.cloned.1.call-start
  224.9 570.8 %all-reduce.5.cloned.1.call-done = (f32[128,128]{1,0:T(8,128)}, f32[512,512]{1,0:T(8,128)}) async-done(((f32[128,128]{1,0:T(8,128)}, f32[512,512]{1,0:T(8,128)}), (f32[128,128]{1,0:T(8,128)}, f32[512,512]{1,0:T(8,128)})) %all-reduce.5.cloned.1.call-update) | async-done | bytes 1114128 | tf_op jit(solution)/shard_map/psum | solution.py:10
  795.7 0.0 all-reduce.7.cloned.1.call-update
  795.7 0.2 reduce-scatter.2.cloned.1.call-start
  795.9 1.9 copy.100
  797.8 1.8 copy.101
  799.6 0.0 reduce-scatter.2.cloned.1.call-update
  799.6 1.4 copy-done.13
  801.0 2.7 fusion.22
  803.7 2.8 copy.90
  806.4 17.9 %all-to-all-start.2 = ((f32[1,128,512,6]{2,0,3,1:T(1,128)}), f32[1,128,512,6]{2,0,3,1:T(1,128)S(1)}, u32[]{:S(2)}, u32[]{:S(2)}) async-start(f32[1,128,512,6]{2,0,3,1:T(1,128)} %copy.90), calls=%async_computation.2 | async-start | bytes 3145728 | tf_op jit(solution)/shard_map/all_to_all | solution.py:71
  824.3 3.0 copy.97
  827.4 36.5 %all-reduce.7.cloned.1.call-done = (f32[128,128]{1,0:T(8,128)}, f32[512,512]{1,0:T(8,128)}) async-done(((f32[128,128]{1,0:T(8,128)}, f32[512,512]{1,0:T(8,128)}), (f32[128,128]{1,0:T(8,128)}, f32[512,512]{1,0:T(8,128)})) %all-reduce.7.cloned.1.call-update) | async-done | bytes 1114128 | tf_op jit(solution)/shard_map/psum | solution.py:10
  863.9 1.5 broadcast_multiply_fusion.1
  865.4 2.3 broadcast_multiply_fusion
  867.7 3.4 copy.124
  871.1 3.4 all_to_all.85
  874.5 3.4 mul.45
  877.9 3.0 copy.106
  881.0 2.0 copy.125
  882.9 2.6 reshape.97
  885.5 1.6 copy.105
  887.2 20.5 %reduce-scatter.2.cloned.1.call-done = f32[32,8,384]{2,1,0:T(8,128)} async-done(((f32[128,8,384]{2,1,0:T(8,128)}), f32[32,8,384]{2,1,0:T(8,128)}) %reduce-scatter.2.cloned.1.call-update) | async-done | bytes 393232 | tf_op jit(solution)/shard_map/reduce_scatter | solution.py:73
  (29 shorter events, 0.1 us)
Async XLA Ops:
  7.2 120.9 %copy-start = (f32[512,512]{1,0:T(8,128)S(1)}, f32[512,512]{1,0:T(8,128)}, u32[]{:S(2)}) copy-start(f32[512,512]{1,0:T(8,128)} %param.11) | copy-start | bytes 3145732
  10.9 52.8 %all-to-all-start.3 = ((f32[1,2,512,384]{2,1,0,3:T(2,128)}), f32[1,2,512,384]{2,1,0,3:T(2,128)S(1)}, u32[]{:S(2)}, u32[]{:S(2)}) async-start(f32[1,2,512,384]{2,1,0,3:T(2,128)} %copy.114), calls=%async_computation.3 | async-start | bytes 3145728 | tf_op jit(solution)/shard_map/all_to_all | solution.py:50
  63.7 9.6 %copy-start.16 = (f32[1,2,512,384]{2,1,0,3:T(2,128)}, f32[1,2,512,384]{2,1,0,3:T(2,128)S(1)}, u32[]{:S(2)}) copy-start(f32[1,2,512,384]{2,1,0,3:T(2,128)S(1)} %all-to-all-done.3) | copy-start | bytes 4718596
  63.7 45.4 %all-to-all-start = ((f32[1,2,512,384]{2,1,0,3:T(2,128)}), f32[1,2,512,384]{2,1,0,3:T(2,128)}, u32[]{:S(2)}, u32[]{:S(2)}) async-start(f32[1,2,512,384]{2,1,0,3:T(2,128)} %copy.113), calls=%async_computation | async-start | bytes 3145728 | tf_op jit(solution)/shard_map/all_to_all | solution.py:60
  109.2 44.6 %all-to-all-start.1 = ((f32[128,8,384]{0,1,2:T(8,128)}), f32[128,8,384]{0,1,2:T(8,128)S(1)}, u32[]{:S(2)}, u32[]{:S(2)}) async-start(f32[128,8,384]{0,1,2:T(8,128)} %copy.87), calls=%async_computation.1 | async-start | bytes 3145728 | tf_op jit(solution)/shard_map/all_to_all | solution.py:51
  128.1 4.2 copy-start.17
  132.3 1.5 copy-start.8
  132.3 2.0 copy-start.6
  134.3 5.3 copy-start.3
  137.0 2.6 copy-start.10
  139.6 1.1 copy-start.1
  153.8 54.7 %all-to-all-start.5 = ((f32[128,512,6]{0,2,1:T(8,128)}), f32[128,512,6]{0,2,1:T(8,128)}, u32[]{:S(2)}, u32[]{:S(2)}) async-start(f32[128,512,6]{0,2,1:T(8,128)} %copy.98), calls=%async_computation.5 | async-start | bytes 4194304 | tf_op jit(solution)/shard_map/all_to_all | solution.py:72
  163.5 1.2 copy-start.14
  167.4 2.8 copy-start.4
  167.4 2.8 copy-start.11
  170.2 2.7 copy-start.2
  170.2 2.7 copy-start.9
  208.5 597.9 %all-to-all-start.4 = ((f32[1,128,512,6]{2,0,3,1:T(1,128)}), f32[1,128,512,6]{2,0,3,1:T(1,128)}, u32[]{:S(2)}, u32[]{:S(2)}) async-start(f32[1,128,512,6]{2,0,3,1:T(1,128)} %copy.95), calls=%async_computation.4 | async-start | bytes 3145728 | tf_op jit(solution)/shard_map/all_to_all | solution.py:57
  215.3 580.3 %all-reduce.5.cloned.1.call-start = ((), (), s32[]{:S(2)}) async-start(), calls=%async_computation.8 | async-start | bytes 2228224 | tf_op jit(solution)/shard_map/psum | solution.py:10
  215.4 3.0 copy-start.7
  215.4 3.0 copy-start.15
  218.4 2.7 copy-start.12
  218.4 2.7 copy-start.5
  224.8 639.1 %all-reduce.7.cloned.1.call-start = ((), (), s32[]{:S(2)}) async-start(), calls=%async_computation.9 | async-start | bytes 2228224 | tf_op jit(solution)/shard_map/psum | solution.py:10
  795.7 111.9 %reduce-scatter.2.cloned.1.call-start = ((), (), s32[]{:S(2)}) async-start(), calls=%async_computation.7 | async-start | bytes 1966080 | tf_op jit(solution)/shard_map/reduce_scatter | solution.py:73
  799.6 1.4 copy-start.13
  806.4 74.5 %all-to-all-start.2 = ((f32[1,128,512,6]{2,0,3,1:T(1,128)}), f32[1,128,512,6]{2,0,3,1:T(1,128)S(1)}, u32[]{:S(2)}, u32[]{:S(2)}) async-start(f32[1,128,512,6]{2,0,3,1:T(1,128)} %copy.90), calls=%async_computation.2 | async-start | bytes 3145728 | tf_op jit(solution)/shard_map/all_to_all | solution.py:71
Sparse Core Ops, SparseCore 0:
  225.0 570.6 all-reduce.4
  798.6 65.2 all-reduce.6
  867.3 40.2 reduce-scatter.1
